TPU v7x, 32 devices: a whole 2x2x4 slice. The times are simulated.
32 devices in a mesh: groups: 2 (over y), dp: 4 (over z), tensor: 2 (over x), store: 2 (over core).
Axes of the slice: x: 2, y: 2, z: 4, core: 2. Of those that a mesh axis runs over, the one named last changes fastest.
Arguments:
- layer_inputs: bfloat16 [8, 32, 128, 4096], P(None, ('groups', 'dp', 'store'), None, 'tensor'), parts along dimension 1, may hold values from -6 to 6
- kv_grads: bfloat16 [8, 2, 32, 128, 1024], P(None, None, ('groups', 'dp', 'store'), None, 'tensor'), parts along dimension 2, may hold values from -6 to 6
- in_proj: bfloat16 [8, 64, 4096], P(None, None, 'tensor'), may hold values from -0.0078125 to 0.0078125
- out_proj: bfloat16 [8, 2, 64, 1024], P(None, None, None, 'tensor'), may hold values from -0.1875 to 0.1875
- owner_map: int32 [16], replicated, may hold values from 0 to 15, each once
Outputs:
- stored_rows: float32 [16, 32, 4096], P('dp', 'groups', ('tensor', 'store')), parts along dimension 1
There are 2 independent parts, one for each index of `groups`. A program takes and returns all parts, laid end to end along the dimension named above; an argument that names none is the same for every part. Nothing has to cross between parts.
Inputs may be any that keep to these rules, and one draw needn't show every extreme that they name: owner_map names every layer block once.
All inputs are finite; a program needn't handle non-finite values.
Results may differ from a plain program's by a relative error of at most 0.0003.
Values sent between devices are 32-bit elements; how exact they have to be, the bound alone decides.
A program may use at most 64 MiB of HBM per device.

v0:
```python
import jax
import jax.numpy as jnp
from jax import lax
from jax.sharding import PartitionSpec as P


def shards(layer_inputs, kv_grads, in_proj, out_proj, owner_map):
    layer_count, examples_dev, seq_len, feature_part = layer_inputs.shape
    rank_size = in_proj.shape[1]
    dp_count = lax.axis_size("dp")
    store_count = lax.axis_size("store")
    tensor_count = lax.axis_size("tensor")
    partial_in = jnp.einsum(
        "lesd,lrd->lesr", layer_inputs, in_proj, preferred_element_type=jnp.float32
    )
    summed = lax.psum(partial_in.reshape(layer_count, examples_dev, seq_len * rank_size), "tensor")
    input_side = summed.reshape(layer_count, examples_dev, seq_len, rank_size)
    partial_out = jnp.einsum(
        "lpesk,lprk->lpesr", kv_grads, out_proj, preferred_element_type=jnp.float32
    )
    gradients = jnp.einsum(
        "lpesr,lesc->elprc", partial_out, input_side, precision=lax.Precision.HIGHEST
    )
    blocks = 2 * layer_count
    gradients = gradients.reshape(examples_dev, blocks, rank_size * rank_size)
    ordered = jnp.take(gradients, owner_map, axis=1)
    row_group = rank_size // (tensor_count * store_count)
    arranged = ordered.reshape(
        examples_dev, blocks, tensor_count, store_count, row_group * rank_size
    )
    arranged = arranged.transpose(0, 1, 3, 2, 4).reshape(
        examples_dev, blocks, rank_size * rank_size
    )
    arrived = lax.all_to_all(
        lax.all_to_all(arranged, "dp", split_axis=1, concat_axis=0, tiled=True),
        "store",
        split_axis=2,
        concat_axis=0,
        tiled=True,
    )
    stored = lax.psum_scatter(arrived, "tensor", scatter_dimension=2, tiled=True)
    per_owner = blocks // dp_count
    row_width = stored.shape[2]
    stored = stored.reshape(store_count, dp_count, examples_dev, per_owner, row_width)
    stored = stored.transpose(3, 1, 0, 2, 4).reshape(
        per_owner, store_count * dp_count * examples_dev, row_width
    )
    return stored


def solution(mesh):
    in_specs = (
        P(None, ("groups", "dp", "store"), None, "tensor"),
        P(None, None, ("groups", "dp", "store"), None, "tensor"),
        P(None, None, "tensor"),
        P(None, None, None, "tensor"),
        P(),
    )
    out_specs = P("dp", "groups", ("tensor", "store"))
    return jax.shard_map(shards, mesh=mesh, in_specs=in_specs, out_specs=out_specs, check_vma=False)
```

profile of v0, /device:TPU:0, one launch (start us, length us, event | category | flops | bytes accessed | tf_op | source)
XLA Modules:
  0.0 141.5 jit_solution(6239306315307151374)
XLA Ops:
  6.5 0.0 copy-start
  6.5 0.0 copy-start.2
  6.5 0.0 copy-start.1
  6.5 0.0 all-reduce.2.cloned.1.call-start
  6.5 1.6 %copy-done = bf16[8,64,2048]{2,1,0:T(8,128)(2,1)S(1)} copy-done((bf16[8,64,2048]{2,1,0:T(8,128)(2,1)S(1)}, bf16[8,64,2048]{2,1,0:T(8,128)(2,1)}, u32[]{:S(2)}) %copy-start) | copy-done | bytes 2097176
  8.1 6.8 %fusion = f32[8,2,128,64]{2,3,0,1:T(8,128)} fusion(bf16[8,2,128,2048]{3,2,1,0:T(8,128)(2,1)} %param.5, bf16[8,64,2048]{2,1,0:T(8,128)(2,1)S(1)} %copy-done), kind=kOutput, calls=%fused_computation.1 | convolution fusion | flops 536870912 | bytes 11010048 | tf_op jit(solution)/shard_map/lesd,lrd->lesr/dot_general | solution.py:13
  15.0 0.0 all-reduce.2.cloned.1.call-update
  15.0 0.0 reduce-scatter.2.cloned.1.call-start
  15.1 0.0 copy-done.2
  15.1 0.0 copy-done.1
  15.1 4.6 %fusion.2 = f32[8,2,2,128,64]{3,4,1,0,2:T(8,128)} fusion(bf16[8,2,2,128,512]{4,3,2,1,0:T(8,128)(2,1)} %param.6, bf16[8,2,64,512]{3,2,1,0:T(8,128)(2,1)S(1)} %copy-done.1), kind=kOutput, calls=%fused_computation.3 | convolution fusion | flops 268435456 | bytes 6291456 | tf_op jit(solution)/shard_map/lpesk,lprk->lpesr/dot_general | solution.py:18
  19.7 26.8 %all-reduce.2.cloned.1.call-done = f32[8,2,128,64]{2,3,0,1:T(8,128)} async-done(((f32[8,2,128,64]{2,3,0,1:T(8,128)}), f32[8,2,128,64]{2,3,0,1:T(8,128)}) %all-reduce.2.cloned.1.call-update) | async-done | bytes 524304 | tf_op jit(solution)/shard_map/psum | solution.py:16
  46.5 2.4 %fusion.6 = f32[2,8,2,64,64]{4,3,2,1,0:T(8,128)S(1)} fusion(f32[8,2,2,128,64]{3,4,1,0,2:T(8,128)} %fusion.2, f32[8,2,128,64]{2,3,0,1:T(8,128)} %all-reduce.2.cloned.1.call-done), kind=kOutput, calls=%fused_computation.7 | convolution fusion | flops 201326592 | bytes 2097152 | tf_op jit(solution)/shard_map/lpesr,lesc->elprc/dot_general | solution.py:21
  48.8 1.1 reshape.27
  50.0 1.4 %copy.44 = f32[2,16,4096]{2,0,1:T(2,128)S(1)} copy(f32[2,16,4096]{2,1,0:T(8,128)} %reshape.27) | data formatting | bytes 1048576 | tf_op jit(solution)/shard_map/reshape | solution.py:25
  51.4 1.1 gather_fusion
  52.6 0.6 gather.7
  53.2 0.3 fusion.8
  53.6 0.5 reshape.28
  54.0 0.4 copy.46
  54.4 18.9 %all_to_all.36 = f32[2,16,4096]{2,0,1:T(2,128)S(1)} all-to-all(f32[2,16,4096]{2,0,1:T(2,128)S(1)} %copy.46), channel_id=1, replica_groups=mesh['groups'=2,'dp'=4,'tensor'=2,'store'=2] {'dp'}, dimensions={1} | all-to-all | bytes 1048576 | tf_op jit(solution)/shard_map/all_to_all | solution.py:35
  73.3 0.3 copy.47
  73.7 5.9 %copy.48 = f32[8,4,4096]{0,1,2:T(4,128)} copy(f32[8,4,4096]{2,1,0:T(4,128)S(1)} %bitcast.36) | data formatting | bytes 1048576 | tf_op jit(solution)/shard_map/all_to_all | solution.py:35
  79.5 12.1 %reshape.44 = f32[2,1,65536]{2,1,0:T(1,128)S(1)} reshape(f32[4096,4,8]{2,1,0:T(4,128)} %bitcast.34) | data formatting | bytes 1048576
  91.6 4.2 %all_to_all.37 = f32[2,1,65536]{2,1,0:T(1,128)S(1)} all-to-all(f32[2,1,65536]{2,1,0:T(1,128)S(1)} %reshape.44), channel_id=1, replica_groups=mesh['groups'=2,'dp'=4,'tensor'=2,'store'=2] {'store'}, dimensions={0} | all-to-all | bytes 1048576 | tf_op jit(solution)/shard_map/all_to_all | solution.py:34
  95.8 0.5 broadcast.17
  96.3 2.3 %reduce = f32[2,65536]{1,0:T(2,128)S(1)} reduce(f32[2,1,65536]{2,1,0:T(1,128)S(1)} %all_to_all.37, f32[]{:T(128)} %broadcast.17), dimensions={1}, to_apply=%all_to_all.30.reduce_sub_computation | reduce | bytes 1048580 | tf_op jit(solution)/shard_map/all_to_all | solution.py:34
  98.6 13.4 %reshape.45 = f32[4096,4,8]{2,1,0:T(4,128)} reshape(f32[2,65536]{1,0:T(2,128)S(1)} %reduce) | data formatting | bytes 1048576
  112.0 6.7 %copy.55 = f32[8,4,2,2048]{3,2,0,1:T(2,128)S(1)} copy(f32[8,4,2,2048]{0,1,3,2:T(4,128)} %bitcast.35) | data formatting | bytes 1048576 | tf_op jit(solution)/shard_map/all_to_all | solution.py:34
  118.7 1.1 copy.64
  119.8 0.0 reduce-scatter.2.cloned.1.call-update
  119.8 12.8 %reduce-scatter.2.cloned.1.call-done = f32[16,4,1024]{2,0,1:T(8,128)} async-done(((f32[16,4,2048]{2,0,1:T(8,128)}), f32[16,4,1024]{2,0,1:T(8,128)}) %reduce-scatter.2.cloned.1.call-update) | async-done | bytes 262160 | tf_op jit(solution)/shard_map/reduce_scatter | solution.py:41
  132.6 1.1 copy.51
  133.8 0.9 copy.53
  (4 shorter events, 0.0 us)
Async XLA Ops:
  6.5 1.6 %copy-start = (bf16[8,64,2048]{2,1,0:T(8,128)(2,1)S(1)}, bf16[8,64,2048]{2,1,0:T(8,128)(2,1)}, u32[]{:S(2)}) copy-start(bf16[8,64,2048]{2,1,0:T(8,128)(2,1)} %param.7) | copy-start | bytes 6291460
  6.5 8.5 %copy-start.2 = (s32[16]{0:T(128)S(1)}, s32[16]{0:T(128)}, u32[]{:S(2)}) copy-start(s32[16]{0:T(128)} %param.9) | copy-start | bytes 196
  6.5 8.6 %copy-start.1 = (bf16[8,2,64,512]{3,2,1,0:T(8,128)(2,1)S(1)}, bf16[8,2,64,512]{3,2,1,0:T(8,128)(2,1)}, u32[]{:S(2)}) copy-start(bf16[8,2,64,512]{3,2,1,0:T(8,128)(2,1)} %param.8) | copy-start | bytes 3145732
  6.5 39.9 %all-reduce.2.cloned.1.call-start = ((), (), s32[]{:S(2)}) async-start(), calls=%async_computation.3 | async-start | bytes 1048576 | tf_op jit(solution)/shard_map/psum | solution.py:16
  15.0 117.6 %reduce-scatter.2.cloned.1.call-start = ((), (), s32[]{:S(2)}) async-start(), calls=%async_computation.4 | async-start | bytes 786432 | tf_op jit(solution)/shard_map/reduce_scatter | solution.py:41
Sparse Core Ops, SparseCore 0:
  15.1 31.2 all-reduce.1
  119.9 12.6 reduce-scatter.1
where the time goes:
time: 142 us; the launch traced here: 141 us
  local copies, waits for them, and re-layouts  48.8 us (34%)
  waiting for transfers between devices  39.6 us (28%)
  blocking collectives  23 us (16%)
  matrix products  13.8 us (10%)
  between operations  13.5 us (10%)
  other arithmetic  2.67 us (2%)
    unnamed x8, local copies, waits for them, and re-layouts  27.1 us
    psum x1, waiting for transfers between devices, shards(): lax.psum(partial_in.reshape(layer_count, examples_dev, seq_len * rank_siz...  26.8 us
    all_to_all x1, blocking collectives, shards(): lax.all_to_all(arranged, 'dp', split_axis=1, concat_axis=0, tiled=True)  18.9 us
    reduce_scatter x1, waiting for transfers between devices, shards(): lax.psum_scatter(arrived, 'tensor', scatter_dimension=2, tiled=True)  12.8 us
    all_to_all x3, local copies, waits for them, and re-layouts, shards(): lax.all_to_all(lax.all_to_all(arranged, 'dp', split_axis=1, concat_axis=0...  8.31 us
    dot_general x1, matrix products, shards(): jnp.einsum('lesd,lrd->lesr', layer_inputs, in_proj, preferred_element_typ...  6.85 us
    all_to_all x2, local copies, waits for them, and re-layouts, shards(): lax.all_to_all(arranged, 'dp', split_axis=1, concat_axis=0, tiled=True)  6.21 us
    dot_general x1, matrix products, shards(): jnp.einsum('lpesk,lprk->lpesr', kv_grads, out_proj, preferred_element_typ...  4.56 us
  transfers between devices with their start and end apart: 2, of which 2 were waited for; matrix products, arithmetic and copies ran while one was open for 3% of the time, Pallas kernels for 0%

commit v1 on v0

v1 whole, which is shorter than its diff:
```python
import functools

import jax
import jax.numpy as jnp
from jax import lax
from jax.experimental import pallas as pl
from jax.experimental.pallas import tpu as pltpu
from jax.sharding import PartitionSpec as P

MESH = pl.DeviceIdType.MESH
AHEAD = 3
LAG = 3


def dot_nt(a, b):
    return lax.dot_general(a, b, (((1,), (1,)), ((), ())), preferred_element_type=jnp.float32)


def split(x):
    high = x.astype(jnp.bfloat16)
    low = (x - high.astype(jnp.float32)).astype(jnp.bfloat16)
    return high, low


def kernel(
    dp, tn, st, owner_ref, x_hbm, kv_hbm, win_hbm, wout_hbm, out_ref,
    x, kv, win, wout, in_part, in_recv, in_terms, out_terms, g_part, g_recv, g_sum,
    load_sem, in_send_sem, in_recv_sem, g_send_sem, g_recv_sem, z_send_sem, z_recv_sem,
):
    layers, examples, seq, features = x.shape
    rank, key_part = wout.shape[2], wout.shape[3]
    blocks = 2 * layers
    per_owner = blocks // dp
    pairs = rank // 2
    quarter = pairs // (tn * st)
    my_z, my_t, my_s = lax.axis_index("dp"), lax.axis_index("tensor"), lax.axis_index("store")
    me = my_z * st + my_s

    def loads(l):
        return (
            pltpu.make_async_copy(win_hbm.at[l], win.at[l], load_sem.at[l, 0]),
            pltpu.make_async_copy(x_hbm.at[l], x.at[l], load_sem.at[l, 1]),
        )

    def out_loads(l):
        return (
            pltpu.make_async_copy(wout_hbm.at[l], wout.at[l], load_sem.at[l, 2]),
            pltpu.make_async_copy(kv_hbm.at[l], kv.at[l], load_sem.at[l, 3]),
        )

    def start(copies):
        for copy in copies:
            copy.start()

    def wait(copies):
        for copy in copies:
            copy.wait()

    for l in range(AHEAD):
        start(loads(l))

    barrier = pltpu.get_barrier_semaphore()
    for d in range(1, tn):
        pl.semaphore_signal(
            barrier, inc=1, device_id={"tensor": lax.rem(my_t + d, tn)}, device_id_type=MESH
        )
    for d in range(1, dp * st):
        other = lax.rem(me + d, dp * st)
        pl.semaphore_signal(
            barrier, inc=1, device_id={"dp": other // st, "store": lax.rem(other, st)}, device_id_type=MESH
        )

    def in_copy(l, d):
        return pltpu.make_async_remote_copy(
            src_ref=in_part.at[l], dst_ref=in_recv.at[l, d - 1],
            send_sem=in_send_sem.at[l, d - 1], recv_sem=in_recv_sem.at[l, d - 1],
            device_id={"tensor": lax.rem(my_t + d, tn)}, device_id_type=MESH,
        )

    for l in range(layers):
        wait(loads(l))
        if l + AHEAD < layers:
            start(loads(l + AHEAD))
        else:
            start(out_loads(l + AHEAD - layers))
        in_part[l] = dot_nt(win[l], x[l].reshape(examples * seq, features))
        if l == 0:
            pl.semaphore_wait(barrier, tn - 1 + dp * st - 1)
        for d in range(1, tn):
            in_copy(l, d).start()

    row = lax.broadcasted_iota(jnp.int32, (rank, rank), 0)
    col = lax.broadcasted_iota(jnp.int32, (rank, rank), 1)
    source = jnp.where(row < pairs, 2 * row, 2 * (row - pairs) + 1)
    reorder = jnp.where(col == source, 1.0, 0.0).astype(jnp.bfloat16)

    for l in range(layers):
        wait(out_loads(l))
        if l + AHEAD < layers:
            start(out_loads(l + AHEAD))
        for p in range(2):
            weight = jnp.dot(reorder, wout[l, p], preferred_element_type=jnp.float32)
            side = dot_nt(weight.astype(jnp.bfloat16), kv[l, p].reshape(examples * seq, key_part))
            high, low = split(side)
            for e in range(examples):
                own = slice(e * seq, (e + 1) * seq)
                out_terms[2 * l + p, e, :, 0:seq] = high[:, own]
                out_terms[2 * l + p, e, :, seq:2 * seq] = high[:, own]
                out_terms[2 * l + p, e, :, 2 * seq:3 * seq] = low[:, own]

    for l in range(layers):
        side = in_part[l]
        for d in range(1, tn):
            in_copy(l, d).wait_recv()
            side = side + in_recv[l, d - 1]
        high, low = split(side)
        for e in range(examples):
            own = slice(e * seq, (e + 1) * seq)
            in_terms[l, e, :, 0:seq] = high[:, own]
            in_terms[l, e, :, seq:2 * seq] = low[:, own]
            in_terms[l, e, :, 2 * seq:3 * seq] = high[:, own]

    def place(n):
        z = lax.rem(my_z + 1 + n % dp, dp)
        k = n // dp
        return z, k, z * per_owner + k

    def g_copy(j, d):
        return pltpu.make_async_remote_copy(
            src_ref=g_part.at[j, lax.rem(my_t + d, tn)], dst_ref=g_recv.at[j, d - 1],
            send_sem=g_send_sem.at[j, d - 1], recv_sem=g_recv_sem.at[j, d - 1],
            device_id={"tensor": lax.rem(my_t + d, tn)}, device_id_type=MESH,
        )

    def z_copy(n, s):
        z, k, j = place(n)
        to = lax.rem(my_s + s, st)
        return pltpu.make_async_remote_copy(
            src_ref=g_sum.at[j, to], dst_ref=out_ref.at[k, me],
            send_sem=z_send_sem.at[j, s], recv_sem=z_recv_sem.at[k, me],
            device_id={"dp": z, "store": to}, device_id_type=MESH,
        )

    def stays(n, s):
        return s == 0 and (n + 1) % dp == 0

    def partial(n):
        _, _, j = place(n)
        block = owner_ref[j]
        for e in range(examples):
            g = dot_nt(out_terms[block, e], in_terms[block // 2, e])
            g = jnp.concatenate([g[:pairs], g[pairs:]], axis=1)
            for c in range(tn * st):
                g_part[j, c // st, c % st, e] = g[c * quarter:(c + 1) * quarter]
        for d in range(1, tn):
            g_copy(j, d).start()

    def total(n):
        _, k, j = place(n)
        whole = g_part[j, my_t]
        for d in range(1, tn):
            g_copy(j, d).wait_recv()
            whole = whole + g_recv[j, d - 1]
        g_sum[j] = whole
        for s in range(st):
            if stays(n, s):
                out_ref[k, me] = g_sum[j, my_s]
            else:
                z_copy(n, s).start()

    for n in range(blocks + LAG):
        if n < blocks:
            partial(n)
        if n >= LAG:
            total(n - LAG)

    for l in range(layers):
        for d in range(1, tn):
            in_copy(l, d).wait_send()
    for n in range(blocks):
        for d in range(1, tn):
            g_copy(place(n)[2], d).wait_send()
        for s in range(st):
            if not stays(n, s):
                z_copy(n, s).wait_send()
    for k in range(per_owner):
        for d in range(1, dp * st):
            other = lax.rem(me + d, dp * st)
            pltpu.make_async_remote_copy(
                src_ref=out_ref.at[k, other], dst_ref=out_ref.at[k, other],
                send_sem=z_send_sem.at[0, 0], recv_sem=z_recv_sem.at[k, other],
                device_id={"dp": other // st, "store": lax.rem(other, st)}, device_id_type=MESH,
            ).wait_recv()


def shards(dp, tn, st, layer_inputs, kv_grads, in_proj, out_proj, owner_map):
    layers, examples, seq, features = layer_inputs.shape
    rank = in_proj.shape[1]
    blocks = 2 * layers
    per_owner = blocks // dp
    quarter = rank // 2 // (tn * st)
    lanes = 2 * rank
    hbm = pl.BlockSpec(memory_space=pltpu.HBM)
    dma = pltpu.SemaphoreType.DMA
    others = max(tn - 1, 1)
    stored = pl.pallas_call(
        functools.partial(kernel, dp, tn, st),
        out_shape=jax.ShapeDtypeStruct((per_owner, dp * st, examples, quarter, lanes), jnp.float32),
        in_specs=[pl.BlockSpec(memory_space=pltpu.SMEM), hbm, hbm, hbm, hbm],
        out_specs=pl.BlockSpec(memory_space=pltpu.VMEM),
        scratch_shapes=[
            pltpu.VMEM(layer_inputs.shape, jnp.bfloat16),
            pltpu.VMEM(kv_grads.shape, jnp.bfloat16),
            pltpu.VMEM(in_proj.shape, jnp.bfloat16),
            pltpu.VMEM(out_proj.shape, jnp.bfloat16),
            pltpu.VMEM((layers, rank, examples * seq), jnp.float32),
            pltpu.VMEM((layers, others, rank, examples * seq), jnp.float32),
            pltpu.VMEM((layers, examples, rank, 3 * seq), jnp.bfloat16),
            pltpu.VMEM((blocks, examples, rank, 3 * seq), jnp.bfloat16),
            pltpu.VMEM((blocks, tn, st, examples, quarter, lanes), jnp.float32),
            pltpu.VMEM((blocks, others, st, examples, quarter, lanes), jnp.float32),
            pltpu.VMEM((blocks, st, examples, quarter, lanes), jnp.float32),
            dma((layers, 4)),
            dma((layers, others)),
            dma((layers, others)),
            dma((blocks, others)),
            dma((blocks, others)),
            dma((blocks, st)),
            dma((per_owner, dp * st)),
        ],
        compiler_params=pltpu.CompilerParams(
            collective_id=0, has_side_effects=True, vmem_limit_bytes=56 * 1024 * 1024
        ),
    )(owner_map, layer_inputs, kv_grads, in_proj, out_proj)
    return stored.reshape(per_owner, dp * st * examples, quarter * lanes)


def solution(mesh):
    in_specs = (
        P(None, ("groups", "dp", "store"), None, "tensor"),
        P(None, None, ("groups", "dp", "store"), None, "tensor"),
        P(None, None, "tensor"),
        P(None, None, None, "tensor"),
        P(),
    )
    out_specs = P("dp", "groups", ("tensor", "store"))
    return jax.shard_map(
        functools.partial(shards, mesh.shape["dp"], mesh.shape["tensor"], mesh.shape["store"]),
        mesh=mesh, in_specs=in_specs, out_specs=out_specs, check_vma=False,
    )
```

time: 142 us -> 38.7 us (0.27)
  local copies, waits for them, and re-layouts: 48.8 us -> 1.7 us
  waiting for transfers between devices: 39.6 us -> 0 us
  Pallas kernels: 0 us -> 36.8 us
  blocking collectives: 23 us -> 0 us
  matrix products: 13.8 us -> 0 us
  between operations: 13.5 us -> 0.01 us
  other arithmetic: 2.67 us -> 0 us
    pallas_call x0 -> x1, Pallas kernels: none -> 36.8 us  [shards(): pl.pallas_call(functools.partial(kernel, dp, tn, st), out_shape=jax.Shape...]
    unnamed x8 -> x0, local copies, waits for them, and re-layouts: 27.1 us -> none
    psum x1 -> x0, waiting for transfers between devices: 26.8 us -> none  [shards(): lax.psum(partial_in.reshape(layer_count, examples_dev, seq_len * rank_siz...]
    all_to_all x2 -> x0, blocking collectives: 23 us -> none  [the longest x1 18.9 us: shards(): lax.all_to_all(arranged, 'dp', split_axis=1, concat_axis=0, tiled=True)]
    all_to_all x5 -> x0, local copies, waits for them, and re-layouts: 14.5 us -> none  [the longest x3 8.31 us: shards(): lax.all_to_all(lax.all_to_all(arranged, 'dp', split_axis=1, concat_axis=0...]
    dot_general x3 -> x0, matrix products: 13.8 us -> none  [the longest x1 6.85 us: shards(): jnp.einsum('lesd,lrd->lesr', layer_inputs, in_proj, preferred_element_typ...]
    reduce_scatter x1 -> x0, waiting for transfers between devices: 12.8 us -> none  [shards(): lax.psum_scatter(arrived, 'tensor', scatter_dimension=2, tiled=True)]
    reshape x5 -> x1, local copies, waits for them, and re-layouts: 4.31 us -> 1.7 us  [shards(): return stored.reshape(per_owner, dp * st * examples, quarter * lanes)]
  transfers between devices with their start and end apart: 2 -> 0, of which waited for: 2 -> 0; matrix products, arithmetic and copies ran while one was open for 3% -> 0% of each run, Pallas kernels for 0% -> 0%
where the time goes in v1:
time: 38.7 us; the launch traced here: 38.5 us
  Pallas kernels  36.8 us (95%)
  local copies, waits for them, and re-layouts  1.7 us (4%)
    pallas_call x1, Pallas kernels, shards(): pl.pallas_call(functools.partial(kernel, dp, tn, st), out_shape=jax.Shape...  36.8 us
    reshape x1, local copies, waits for them, and re-layouts, shards(): return stored.reshape(per_owner, dp * st * examples, quarter * lanes)  1.7 us

profile of v1, /device:TPU:0, one launch (start us, length us, event | category | flops | bytes accessed | tf_op | source)
XLA Modules:
  0.0 38.5 jit_solution(4663281184596707002)
XLA Ops:
  0.0 36.8 %shard_map.55 = f32[4,8,2,8,128]{4,3,2,1,0:T(8,128)} custom-call(s32[16]{0:T(128)} %owner_ref.1, bf16[8,2,128,2048]{3,2,1,0:T(8,128)(2,1)} %x_hbm.1, bf16[8,2,2,128,512]{4,3,2,1,0:T(8,128)(2,1)} %kv_hbm.1, bf16[8,64,2048]{2,1,0:T(8,128)(2,1)} %win_hbm.1, bf16[8,2,64,512]{3,2,1,0:T(8,128)(2,1)} %wout_hbm.1), custom_call_target="tpu_custom_call" | custom-call | tf_op jit(solution)/shard_map/pallas_call | solution.py:206
  36.8 1.7 %reshape.3 = f32[4,16,1024]{2,1,0:T(8,128)} reshape(f32[4,8,2,8,128]{4,3,2,1,0:T(8,128)} %shard_map.55) | data formatting | bytes 524288 | tf_op jit(solution)/shard_map/reshape | solution.py:235

commit v2 on v1

--- a/solution.py
+++ b/solution.py
@@ -9,7 +9,6 @@
 
 MESH = pl.DeviceIdType.MESH
 AHEAD = 3
-LAG = 3
 
 
 def dot_nt(a, b):
@@ -33,6 +32,8 @@
     per_owner = blocks // dp
     pairs = rank // 2
     quarter = pairs // (tn * st)
+    halves = 2 if dp % 2 == 0 else 1
+    half = dp // halves
     my_z, my_t, my_s = lax.axis_index("dp"), lax.axis_index("tensor"), lax.axis_index("store")
     me = my_z * st + my_s
 
@@ -121,8 +122,9 @@
             in_terms[l, e, :, 2 * seq:3 * seq] = high[:, own]
 
     def place(n):
-        z = lax.rem(my_z + 1 + n % dp, dp)
-        k = n // dp
+        turn, k = n // per_owner, n % per_owner
+        side = lax.rem(my_z // half + 1 + turn // half, halves)
+        z = side * half + lax.rem(my_z + 1 + turn, half)
         return z, k, z * per_owner + k
 
     def g_copy(j, d):
@@ -142,7 +144,7 @@
         )
 
     def stays(n, s):
-        return s == 0 and (n + 1) % dp == 0
+        return s == 0 and n // per_owner == dp - 1
 
     def partial(n):
         _, _, j = place(n)
@@ -168,11 +170,10 @@
             else:
                 z_copy(n, s).start()
 
-    for n in range(blocks + LAG):
-        if n < blocks:
-            partial(n)
-        if n >= LAG:
-            total(n - LAG)
+    for n in range(blocks):
+        partial(n)
+    for n in range(blocks):
+        total(n)
 
     for l in range(layers):
         for d in range(1, tn):

time: 38.7 us -> 33.7 us (0.87)
  Pallas kernels: 36.8 us -> 31.8 us
    pallas_call x1, Pallas kernels: 36.8 us -> 31.8 us  [shards(): pl.pallas_call(functools.partial(kernel, dp, tn, st), out_shape=jax.Shape...]
where the time goes in v2:
time: 33.7 us; the launch traced here: 33.5 us
  Pallas kernels  31.8 us (94%)
  local copies, waits for them, and re-layouts  1.7 us (5%)
    pallas_call x1, Pallas kernels, shards(): pl.pallas_call(functools.partial(kernel, dp, tn, st), out_shape=jax.Shape...  31.8 us
    reshape x1, local copies, waits for them, and re-layouts, shards(): return stored.reshape(per_owner, dp * st * examples, quarter * lanes)  1.7 us

profile of v2, /device:TPU:0, one launch (start us, length us, event | category | flops | bytes accessed | tf_op | source)
XLA Modules:
  0.0 33.5 jit_solution(4814110302858740093)
XLA Ops:
  0.0 31.8 %shard_map.55 = f32[4,8,2,8,128]{4,3,2,1,0:T(8,128)} custom-call(s32[16]{0:T(128)} %owner_ref.1, bf16[8,2,128,2048]{3,2,1,0:T(8,128)(2,1)} %x_hbm.1, bf16[8,2,2,128,512]{4,3,2,1,0:T(8,128)(2,1)} %kv_hbm.1, bf16[8,64,2048]{2,1,0:T(8,128)(2,1)} %win_hbm.1, bf16[8,2,64,512]{3,2,1,0:T(8,128)(2,1)} %wout_hbm.1), custom_call_target="tpu_custom_call" | custom-call | tf_op jit(solution)/shard_map/pallas_call | solution.py:207
  31.8 1.7 %reshape.3 = f32[4,16,1024]{2,1,0:T(8,128)} reshape(f32[4,8,2,8,128]{4,3,2,1,0:T(8,128)} %shard_map.55) | data formatting | bytes 524288 | tf_op jit(solution)/shard_map/reshape | solution.py:236
